TPU v7x, 128 devices: a whole 4x4x4 slice. The times are simulated.
128 devices in a mesh: section: 8 (over y, core), dp: 16 (over z, x).
Axes of the slice: x: 4, y: 4, z: 4, core: 2. Of those that a mesh axis runs over, the one named last changes fastest.
Arguments:
- hidden: bfloat16 [4, 576, 8192], P(None, 'dp'), may hold values from -6 to 6
- lengths: int32 [4, 16], replicated, may hold values from 1 to 36, 256 in all within a row
- response_mask: int32 [4, 576], replicated, may hold values 0 or 1
- norm_gain: float32 [8, 8192], P('section'), may hold values from 0.25 to 1.75
- weight_in: bfloat16 [8, 8192, 256], P('section'), may hold values from -0.0625 to 0.0625
- weight_out: bfloat16 [8, 256, 8192], P('section'), may hold values from -0.375 to 0.375
- final_gain: float32 [8192], replicated, may hold values from 0.25 to 1.75
- value_heads: float32 [3, 8192], replicated, may hold values from -0.0625 to 0.0625
- old_values: float32 [3, 4, 576], replicated, may hold values from -6 to 6
- advantages: float32 [3, 4, 576], replicated, may hold values from -6 to 6
- multipliers: float32 [2], replicated, may hold values from 0.5 to 4
Outputs:
- grad_in: float32 [8, 8192, 256], P('section', 'dp')
- grad_out: float32 [8, 256, 8192], P('section', None, 'dp')
- objective: float32 [], replicated
Inputs may be any that keep to these rules, and one draw needn't show every extreme that they name: In every micro-batch the 16 lengths sum to 256 and the longest equals 36.
All inputs are finite; a program needn't handle non-finite values.
Results may differ from a plain program's by a relative error of at most 0.034.
Values may be sent and summed in bfloat16 or wider, within the bound.
A program may use at most 128 MiB of HBM per device.

v0:
```python
import jax
import jax.numpy as jnp
from jax import lax
from jax.sharding import PartitionSpec as P

BAL = 16


epsilon = 1e-05
loss_scale = 4096.0


def from_behind(shard, axis, by):
    count = lax.axis_size(axis)
    pairs = [(i, i + by) for i in range(count) if 0 <= i + by < count]
    return lax.ppermute(shard, axis, pairs)


def rms_factor(values):
    return lax.rsqrt(jnp.mean(values * values, axis=-1, keepdims=True) + epsilon)


def norm_backward(grad_normed, values, factor, scale):
    scaled = grad_normed * scale
    centred = jnp.mean(scaled * values, axis=-1, keepdims=True)
    return factor * scaled - values * (factor * factor * factor) * centred


def layer_forward(block_in, norm_scale, matrix_in, matrix_out):
    values = block_in.astype(jnp.float32)
    factor = rms_factor(values)
    normed = (values * factor * norm_scale).astype(jnp.bfloat16)
    hidden_pre = jnp.dot(normed, matrix_in, preferred_element_type=jnp.float32)
    activated = (hidden_pre * jax.nn.sigmoid(hidden_pre)).astype(jnp.bfloat16)
    mixed = values + jnp.dot(activated, matrix_out, preferred_element_type=jnp.float32)
    return (mixed.astype(jnp.bfloat16), hidden_pre)


def layer_backward(block_in, hidden_pre, grad_rows, norm_scale, matrix_in, matrix_out):
    values = block_in.astype(jnp.float32)
    factor = rms_factor(values)
    normed = (values * factor * norm_scale).astype(jnp.bfloat16)
    sigmoid_pre = jax.nn.sigmoid(hidden_pre)
    activated = (hidden_pre * sigmoid_pre).astype(jnp.bfloat16)
    grad_act = lax.dot_general(
        grad_rows, matrix_out, (((1,), (1,)), ((), ())), preferred_element_type=jnp.float32
    )
    grad_matrix_out = lax.dot_general(
        activated, grad_rows, (((0,), (0,)), ((), ())), preferred_element_type=jnp.float32
    )
    grad_pre = (grad_act * sigmoid_pre * (1.0 + hidden_pre * (1.0 - sigmoid_pre))).astype(
        jnp.bfloat16
    )
    grad_matrix_in = lax.dot_general(
        normed, grad_pre, (((0,), (0,)), ((), ())), preferred_element_type=jnp.float32
    )
    grad_normed = lax.dot_general(
        grad_pre, matrix_in, (((1,), (1,)), ((), ())), preferred_element_type=jnp.float32
    )
    grad_block = grad_rows.astype(jnp.float32) + norm_backward(
        grad_normed, values, factor, norm_scale
    )
    return (grad_block.astype(jnp.bfloat16), grad_matrix_in, grad_matrix_out)


def head_gradient(block_out, final_gain, value_heads, targets, weights, coefficients, grad_scale):
    values = block_out.astype(jnp.float32)
    factor = rms_factor(values)
    normed = values * factor * final_gain
    estimates = lax.dot_general(
        value_heads,
        normed,
        (((1,), (1,)), ((), ())),
        precision=lax.Precision.HIGHEST,
        preferred_element_type=jnp.float32,
    )
    errors = estimates - targets
    weighted = coefficients[:, None] * weights[None, :] * errors
    loss_part = 0.5 * jnp.sum(weighted * errors)
    grad_normed = lax.dot_general(
        weighted * grad_scale,
        value_heads,
        (((0,), (0,)), ((), ())),
        precision=lax.Precision.HIGHEST,
        preferred_element_type=jnp.float32,
    )
    start_grad = norm_backward(grad_normed, values, factor, final_gain).astype(jnp.bfloat16)
    return (loss_part, start_grad)


def local(
    hidden,
    lengths,
    response_mask,
    norm_gain,
    weight_in,
    weight_out,
    final_gain,
    value_heads,
    old_values,
    advantages,
    multipliers,
):
    shard_count = lax.axis_size("dp")
    section_count = lax.axis_size("section")
    shard_index = lax.axis_index("dp")
    section_index = lax.axis_index("section")
    micro_count = hidden.shape[0]
    capacity = hidden.shape[1]
    width = hidden.shape[2]
    norm_scale = norm_gain[0]
    matrix_in = weight_in[0]
    matrix_out = weight_out[0]
    coefficients = jnp.concatenate([jnp.ones((1,), jnp.float32), multipliers])
    token_count = micro_count * BAL * shard_count
    grad_scale = loss_scale / token_count
    targets_all = old_values + advantages
    offsets = jnp.arange(capacity, dtype=jnp.int32)
    own_lengths = jnp.take(lengths, shard_index, axis=1)
    live_rows = offsets[None, :] < own_lengths[:, None]
    row_ids = jnp.broadcast_to(shard_index * capacity + offsets[None, :], (micro_count, capacity))
    weights = (
        jnp.take_along_axis(response_mask, row_ids, axis=1) * live_rows.astype(jnp.int32)
    ).astype(jnp.float32)
    head_count = targets_all.shape[0]
    targets = jnp.take_along_axis(
        targets_all, jnp.broadcast_to(row_ids[None], (head_count,) + row_ids.shape), axis=2
    )
    batch_count = hidden.shape[0]
    block_rows = hidden.shape[1]
    adapter_width = matrix_in.shape[1]
    is_first = section_index == 0
    is_last = section_index == section_count - 1
    tick_count = batch_count + section_count - 1

    def forward_tick(tick, carried):
        incoming, stash_rows, stash_pre, start_rows, loss_sum = carried
        micro_now = tick - section_index
        active = (micro_now >= 0) & (micro_now < batch_count)
        micro_slot = jnp.clip(micro_now, 0, batch_count - 1)
        block_in = jnp.where(
            is_first, lax.dynamic_index_in_dim(hidden, micro_slot, 0, keepdims=False), incoming
        )

        def forward_compute(buffers):
            stash_now, pre_now, starts_now, loss_now = buffers
            block_out, hidden_pre = layer_forward(block_in, norm_scale, matrix_in, matrix_out)
            stash_now = lax.dynamic_update_index_in_dim(stash_now, block_in, micro_slot, 0)
            pre_now = lax.dynamic_update_index_in_dim(pre_now, hidden_pre, micro_slot, 0)

            def finish(pending):
                starts_held, loss_held = pending
                loss_part, start_grad = head_gradient(
                    block_out,
                    final_gain,
                    value_heads,
                    lax.dynamic_index_in_dim(targets, micro_slot, 1, keepdims=False),
                    lax.dynamic_index_in_dim(weights, micro_slot, 0, keepdims=False),
                    coefficients,
                    grad_scale,
                )
                return (
                    lax.dynamic_update_index_in_dim(starts_held, start_grad, micro_slot, 0),
                    loss_held + loss_part,
                )

            def passing(pending):
                return pending

            starts_now, loss_now = lax.cond(is_last, finish, passing, (starts_now, loss_now))
            return (block_out, (stash_now, pre_now, starts_now, loss_now))

        def forward_unchanged(buffers):
            return (jnp.zeros_like(block_in), buffers)

        block_out, buffers = lax.cond(
            active,
            forward_compute,
            forward_unchanged,
            (stash_rows, stash_pre, start_rows, loss_sum),
        )
        incoming = from_behind(block_out, "section", 1)
        return (incoming,) + buffers

    forward_start = (
        jnp.zeros((block_rows, width), jnp.bfloat16),
        jnp.zeros((batch_count, block_rows, width), jnp.bfloat16),
        jnp.zeros((batch_count, block_rows, adapter_width), jnp.float32),
        jnp.zeros((batch_count, block_rows, width), jnp.bfloat16),
        jnp.zeros((), jnp.float32),
    )
    forward_done = lax.fori_loop(0, tick_count, forward_tick, forward_start)
    stash_rows, stash_pre, start_rows, loss_sum = (
        forward_done[1],
        forward_done[2],
        forward_done[3],
        forward_done[4],
    )

    def backward_tick(tick, carried):
        incoming, grad_in_sum, grad_out_sum = carried
        micro_now = tick - (section_count - 1 - section_index)
        active = (micro_now >= 0) & (micro_now < batch_count)
        micro_slot = jnp.clip(micro_now, 0, batch_count - 1)
        grad_rows = jnp.where(
            is_last, lax.dynamic_index_in_dim(start_rows, micro_slot, 0, keepdims=False), incoming
        )

        def backward_compute(sums):
            grad_block, grad_matrix_in, grad_matrix_out = layer_backward(
                lax.dynamic_index_in_dim(stash_rows, micro_slot, 0, keepdims=False),
                lax.dynamic_index_in_dim(stash_pre, micro_slot, 0, keepdims=False),
                grad_rows,
                norm_scale,
                matrix_in,
                matrix_out,
            )
            return (grad_block, (sums[0] + grad_matrix_in, sums[1] + grad_matrix_out))

        def backward_unchanged(sums):
            return (jnp.zeros_like(grad_rows), sums)

        grad_block, sums = lax.cond(
            active, backward_compute, backward_unchanged, (grad_in_sum, grad_out_sum)
        )
        incoming = from_behind(grad_block, "section", -1)
        return (incoming,) + sums

    backward_start = (
        jnp.zeros((block_rows, width), jnp.bfloat16),
        jnp.zeros(matrix_in.shape, jnp.float32),
        jnp.zeros(matrix_out.shape, jnp.float32),
    )
    backward_done = lax.fori_loop(0, tick_count, backward_tick, backward_start)
    grad_in_sum, grad_out_sum = (backward_done[1], backward_done[2])
    grad_in_part, grad_out_part = (
        lax.psum_scatter(
            grad_in_sum.astype(jnp.bfloat16), "dp", scatter_dimension=0, tiled=True
        ).astype(jnp.float32),
        lax.psum_scatter(
            grad_out_sum.astype(jnp.bfloat16), "dp", scatter_dimension=1, tiled=True
        ).astype(jnp.float32),
    )
    loss_local = jnp.where(is_last, loss_sum, jnp.zeros_like(loss_sum))
    objective = lax.psum(loss_local, ("section", "dp")) / token_count
    return (grad_in_part[None], grad_out_part[None], objective)


def solution(mesh):
    return jax.shard_map(
        local,
        mesh=mesh,
        in_specs=(
            P(None, "dp", None),
            P(),
            P(),
            P("section", None),
            P("section", None, None),
            P("section", None, None),
            P(),
            P(),
            P(),
            P(),
            P(),
        ),
        out_specs=(P("section", "dp", None), P("section", None, "dp"), P()),
        check_vma=False,
    )
```

profile of v0, /device:TPU:1, one launch (start us, length us, event | category | flops | bytes accessed | tf_op | source)
XLA Modules:
  0.0 673.8 jit_solution(7881553626704809058)
XLA Ops:
  24.7 172.2 %while.41 = (s32[]{:T(128)}, bf16[36,8192]{1,0:T(8,128)(2,1)S(1)}, bf16[4,36,8192]{2,1,0:T(8,128)(2,1)S(1)}, f32[4,36,256]{2,1,0:T(8,128)}, bf16[4,36,8192]{2,1,...) while((s32[]{:T(128)}, bf16[36,8192]{1,0:T(8,128)(2,1)S(1)}, ...), condition=%wide.region_9.10_spmd, body=%wide.region_0.9_spmd.sunk | while | flops 331233280 | bytes 38294696 | solution.py:192
  30.2 7.8 %collective-permute-done = bf16[36,8192]{1,0:T(8,128)(2,1)S(1)} collective-permute-done((bf16[36,8192]{1,0:T(8,128)(2,1)}, bf16[36,8192]{1,0:T(8,128)(2,1)S(1)}, u32[]{:S(2)}, u32[]{:S(2)}) %collective-permute-start) | collective-permute-done | bytes 589856 | tf_op jit(solution)/shard_map/while/body/eval_jaxpr/ppermute | solution.py:16
  47.1 7.8 %collective-permute-done = bf16[36,8192]{1,0:T(8,128)(2,1)S(1)} collective-permute-done((bf16[36,8192]{1,0:T(8,128)(2,1)}, bf16[36,8192]{1,0:T(8,128)(2,1)S(1)}, u32[]{:S(2)}, u32[]{:S(2)}) %collective-permute-start) | collective-permute-done | bytes 589856 | tf_op jit(solution)/shard_map/while/body/eval_jaxpr/ppermute | solution.py:16
  66.4 7.8 %collective-permute-done = bf16[36,8192]{1,0:T(8,128)(2,1)S(1)} collective-permute-done((bf16[36,8192]{1,0:T(8,128)(2,1)}, bf16[36,8192]{1,0:T(8,128)(2,1)S(1)}, u32[]{:S(2)}, u32[]{:S(2)}) %collective-permute-start) | collective-permute-done | bytes 589856 | tf_op jit(solution)/shard_map/while/body/eval_jaxpr/ppermute | solution.py:16
  113.5 10.5 %collective-permute-start = (bf16[36,8192]{1,0:T(8,128)(2,1)}, bf16[36,8192]{1,0:T(8,128)(2,1)S(1)}, u32[]{:S(2)}, u32[]{:S(2)}) collective-permute-start(bf16[36,8192]{1,0:T(8,128)(2,1)} %get-tuple-element.1237), channel_id=1, source_target_pairs={{0,16},{16,32},{32,48},{48,64},{64,80},{80,96},{96,112},{1,17},{17... | collective-permute-start | bytes 1769480 | tf_op jit(solution)/shard_map/while/body/eval_jaxpr/ppermute | solution.py:16
  176.1 7.8 %collective-permute-done = bf16[36,8192]{1,0:T(8,128)(2,1)S(1)} collective-permute-done((bf16[36,8192]{1,0:T(8,128)(2,1)}, bf16[36,8192]{1,0:T(8,128)(2,1)S(1)}, u32[]{:S(2)}, u32[]{:S(2)}) %collective-permute-start) | collective-permute-done | bytes 589856 | tf_op jit(solution)/shard_map/while/body/eval_jaxpr/ppermute | solution.py:16
  204.9 296.7 %while.42 = (s32[]{:T(128)}, bf16[36,8192]{1,0:T(8,128)(2,1)S(1)}, f32[8192,256]{1,0:T(8,128)}, f32[256,8192]{1,0:T(8,128)}, s32[]{:T(128)}, /*index=5*/pred[]{:...) while((s32[]{:T(128)}, bf16[36,8192]{1,0:T(8,128)(2,1)S(1)}, ...), condition=%wide.region_15.16_spmd, body=%wide.region_10.15_spmd.sunk | while | flops 613906560 | bytes 195500496 | solution.py:234
  207.7 10.8 %collective-permute-done.1 = bf16[36,8192]{1,0:T(8,128)(2,1)S(1)} collective-permute-done((bf16[36,8192]{1,0:T(8,128)(2,1)}, bf16[36,8192]{1,0:T(8,128)(2,1)S(1)}, u32[]{:S(2)}, u32[]{:S(2)}) %collective-permute-start.1) | collective-permute-done | bytes 589856 | tf_op jit(solution)/shard_map/while/body/eval_jaxpr/ppermute | solution.py:16
  221.4 10.2 %collective-permute-done.1 = bf16[36,8192]{1,0:T(8,128)(2,1)S(1)} collective-permute-done((bf16[36,8192]{1,0:T(8,128)(2,1)}, bf16[36,8192]{1,0:T(8,128)(2,1)S(1)}, u32[]{:S(2)}, u32[]{:S(2)}) %collective-permute-start.1) | collective-permute-done | bytes 589856 | tf_op jit(solution)/shard_map/while/body/eval_jaxpr/ppermute | solution.py:16
  234.4 10.2 %collective-permute-done.1 = bf16[36,8192]{1,0:T(8,128)(2,1)S(1)} collective-permute-done((bf16[36,8192]{1,0:T(8,128)(2,1)}, bf16[36,8192]{1,0:T(8,128)(2,1)S(1)}, u32[]{:S(2)}, u32[]{:S(2)}) %collective-permute-start.1) | collective-permute-done | bytes 589856 | tf_op jit(solution)/shard_map/while/body/eval_jaxpr/ppermute | solution.py:16
  247.4 10.2 %collective-permute-done.1 = bf16[36,8192]{1,0:T(8,128)(2,1)S(1)} collective-permute-done((bf16[36,8192]{1,0:T(8,128)(2,1)}, bf16[36,8192]{1,0:T(8,128)(2,1)S(1)}, u32[]{:S(2)}, u32[]{:S(2)}) %collective-permute-start.1) | collective-permute-done | bytes 589856 | tf_op jit(solution)/shard_map/while/body/eval_jaxpr/ppermute | solution.py:16
  260.4 10.2 %collective-permute-done.1 = bf16[36,8192]{1,0:T(8,128)(2,1)S(1)} collective-permute-done((bf16[36,8192]{1,0:T(8,128)(2,1)}, bf16[36,8192]{1,0:T(8,128)(2,1)S(1)}, u32[]{:S(2)}, u32[]{:S(2)}) %collective-permute-start.1) | collective-permute-done | bytes 589856 | tf_op jit(solution)/shard_map/while/body/eval_jaxpr/ppermute | solution.py:16
  273.4 96.0 %collective-permute-done.1 = bf16[36,8192]{1,0:T(8,128)(2,1)S(1)} collective-permute-done((bf16[36,8192]{1,0:T(8,128)(2,1)}, bf16[36,8192]{1,0:T(8,128)(2,1)S(1)}, u32[]{:S(2)}, u32[]{:S(2)}) %collective-permute-start.1) | collective-permute-done | bytes 589856 | tf_op jit(solution)/shard_map/while/body/eval_jaxpr/ppermute | solution.py:16
  369.4 17.6 %conditional.6 = (bf16[36,8192]{1,0:T(8,128)(2,1)}, f32[8192,256]{1,0:T(8,128)}, f32[256,8192]{1,0:T(8,128)}) conditional(s32[]{:T(128)} %convert_element_type.169, (f32[8192,256]{1,0:T(8,128)}, f32[256,8192]{1,0:T(8,128)}) %tuple.125, (pred[]{:T(512)}, s32[]{:T(128)}, bf16[4,36,8192]{2,1,0:T(8,128)(2,1)}, bf16[36,8192]{1,0:T(8,128)(2,1)S(1)}, ...), branch_computations={%region_11.11_spmd, %region_12.14_spmd} | conditional | flops 613906560 | bytes 193140864 | solution.py:223
  388.9 10.2 %collective-permute-done.1 = bf16[36,8192]{1,0:T(8,128)(2,1)S(1)} collective-permute-done((bf16[36,8192]{1,0:T(8,128)(2,1)}, bf16[36,8192]{1,0:T(8,128)(2,1)S(1)}, u32[]{:S(2)}, u32[]{:S(2)}) %collective-permute-start.1) | collective-permute-done | bytes 589856 | tf_op jit(solution)/shard_map/while/body/eval_jaxpr/ppermute | solution.py:16
  399.0 17.6 %conditional.6 = (bf16[36,8192]{1,0:T(8,128)(2,1)}, f32[8192,256]{1,0:T(8,128)}, f32[256,8192]{1,0:T(8,128)}) conditional(s32[]{:T(128)} %convert_element_type.169, (f32[8192,256]{1,0:T(8,128)}, f32[256,8192]{1,0:T(8,128)}) %tuple.125, (pred[]{:T(512)}, s32[]{:T(128)}, bf16[4,36,8192]{2,1,0:T(8,128)(2,1)}, bf16[36,8192]{1,0:T(8,128)(2,1)S(1)}, ...), branch_computations={%region_11.11_spmd, %region_12.14_spmd} | conditional | flops 613906560 | bytes 193140864 | solution.py:223
  418.5 10.2 %collective-permute-done.1 = bf16[36,8192]{1,0:T(8,128)(2,1)S(1)} collective-permute-done((bf16[36,8192]{1,0:T(8,128)(2,1)}, bf16[36,8192]{1,0:T(8,128)(2,1)S(1)}, u32[]{:S(2)}, u32[]{:S(2)}) %collective-permute-start.1) | collective-permute-done | bytes 589856 | tf_op jit(solution)/shard_map/while/body/eval_jaxpr/ppermute | solution.py:16
  428.7 17.6 %conditional.6 = (bf16[36,8192]{1,0:T(8,128)(2,1)}, f32[8192,256]{1,0:T(8,128)}, f32[256,8192]{1,0:T(8,128)}) conditional(s32[]{:T(128)} %convert_element_type.169, (f32[8192,256]{1,0:T(8,128)}, f32[256,8192]{1,0:T(8,128)}) %tuple.125, (pred[]{:T(512)}, s32[]{:T(128)}, bf16[4,36,8192]{2,1,0:T(8,128)(2,1)}, bf16[36,8192]{1,0:T(8,128)(2,1)S(1)}, ...), branch_computations={%region_11.11_spmd, %region_12.14_spmd} | conditional | flops 613906560 | bytes 193140864 | solution.py:223
  448.2 10.2 %collective-permute-done.1 = bf16[36,8192]{1,0:T(8,128)(2,1)S(1)} collective-permute-done((bf16[36,8192]{1,0:T(8,128)(2,1)}, bf16[36,8192]{1,0:T(8,128)(2,1)S(1)}, u32[]{:S(2)}, u32[]{:S(2)}) %collective-permute-start.1) | collective-permute-done | bytes 589856 | tf_op jit(solution)/shard_map/while/body/eval_jaxpr/ppermute | solution.py:16
  458.4 17.6 %conditional.6 = (bf16[36,8192]{1,0:T(8,128)(2,1)}, f32[8192,256]{1,0:T(8,128)}, f32[256,8192]{1,0:T(8,128)}) conditional(s32[]{:T(128)} %convert_element_type.169, (f32[8192,256]{1,0:T(8,128)}, f32[256,8192]{1,0:T(8,128)}) %tuple.125, (pred[]{:T(512)}, s32[]{:T(128)}, bf16[4,36,8192]{2,1,0:T(8,128)(2,1)}, bf16[36,8192]{1,0:T(8,128)(2,1)S(1)}, ...), branch_computations={%region_11.11_spmd, %region_12.14_spmd} | conditional | flops 613906560 | bytes 193140864 | solution.py:223
  477.9 10.2 %collective-permute-done.1 = bf16[36,8192]{1,0:T(8,128)(2,1)S(1)} collective-permute-done((bf16[36,8192]{1,0:T(8,128)(2,1)}, bf16[36,8192]{1,0:T(8,128)(2,1)S(1)}, u32[]{:S(2)}, u32[]{:S(2)}) %collective-permute-start.1) | collective-permute-done | bytes 589856 | tf_op jit(solution)/shard_map/while/body/eval_jaxpr/ppermute | solution.py:16
  489.0 10.7 %collective-permute-start.1 = (bf16[36,8192]{1,0:T(8,128)(2,1)}, bf16[36,8192]{1,0:T(8,128)(2,1)S(1)}, u32[]{:S(2)}, u32[]{:S(2)}) collective-permute-start(bf16[36,8192]{1,0:T(8,128)(2,1)} %get-tuple-element.1254), channel_id=1, source_target_pairs={{16,0},{32,16},{48,32},{64,48},{80,64},{96,80},{112,96},{17,1},{33... | collective-permute-start | bytes 1769480 | tf_op jit(solution)/shard_map/while/body/eval_jaxpr/ppermute | solution.py:16
  513.3 66.7 %psum.7 = f32[]{:T(128)} all-reduce(f32[]{:T(128)S(6)} %select_n.142), channel_id=1, replica_groups=mesh['section'=8,'dp'=16] {'section','dp'}, use_global_device_ids=true, to_apply=%region_18.19 | all-reduce | flops 1 | bytes 8 | tf_op jit(solution)/shard_map/psum | solution.py:245
  585.0 79.0 %reduce-scatter.5.cloned.1.call-done = bf16[256,512]{1,0:T(8,128)(2,1)} async-done(((bf16[256,8192]{1,0:T(8,128)(2,1)}), bf16[256,512]{1,0:T(8,128)(2,1)}) %reduce-scatter.5.cloned.1.call-update) | async-done | bytes 262160 | tf_op jit(solution)/shard_map/reduce_scatter | solution.py:240
  (221 shorter events, 311.7 us)
Async XLA Ops:
  7.2 576.1 %reduce-scatter.3.cloned.1.call-start = ((), (), s32[]{:S(2)}) async-start(), calls=%async_computation.2 | async-start | bytes 4456448 | tf_op jit(solution)/shard_map/reduce_scatter | solution.py:237
  25.7 12.4 %collective-permute-start = (bf16[36,8192]{1,0:T(8,128)(2,1)}, bf16[36,8192]{1,0:T(8,128)(2,1)S(1)}, u32[]{:S(2)}, u32[]{:S(2)}) collective-permute-start(bf16[36,8192]{1,0:T(8,128)(2,1)} %get-tuple-element.1237), channel_id=1, source_target_pairs={{0,16},{16,32},{32,48},{48,64},{64,80},{80,96},{96,112},{1,17},{17... | collective-permute-start | bytes 1769480 | tf_op jit(solution)/shard_map/while/body/eval_jaxpr/ppermute | solution.py:16
  45.2 9.7 %collective-permute-start = (bf16[36,8192]{1,0:T(8,128)(2,1)}, bf16[36,8192]{1,0:T(8,128)(2,1)S(1)}, u32[]{:S(2)}, u32[]{:S(2)}) collective-permute-start(bf16[36,8192]{1,0:T(8,128)(2,1)} %get-tuple-element.1237), channel_id=1, source_target_pairs={{0,16},{16,32},{32,48},{48,64},{64,80},{80,96},{96,112},{1,17},{17... | collective-permute-start | bytes 1769480 | tf_op jit(solution)/shard_map/while/body/eval_jaxpr/ppermute | solution.py:16
  62.1 12.1 %collective-permute-start = (bf16[36,8192]{1,0:T(8,128)(2,1)}, bf16[36,8192]{1,0:T(8,128)(2,1)S(1)}, u32[]{:S(2)}, u32[]{:S(2)}) collective-permute-start(bf16[36,8192]{1,0:T(8,128)(2,1)} %get-tuple-element.1237), channel_id=1, source_target_pairs={{0,16},{16,32},{32,48},{48,64},{64,80},{80,96},{96,112},{1,17},{17... | collective-permute-start | bytes 1769480 | tf_op jit(solution)/shard_map/while/body/eval_jaxpr/ppermute | solution.py:16
  81.3 12.1 %collective-permute-start = (bf16[36,8192]{1,0:T(8,128)(2,1)}, bf16[36,8192]{1,0:T(8,128)(2,1)S(1)}, u32[]{:S(2)}, u32[]{:S(2)}) collective-permute-start(bf16[36,8192]{1,0:T(8,128)(2,1)} %get-tuple-element.1237), channel_id=1, source_target_pairs={{0,16},{16,32},{32,48},{48,64},{64,80},{80,96},{96,112},{1,17},{17... | collective-permute-start | bytes 1769480 | tf_op jit(solution)/shard_map/while/body/eval_jaxpr/ppermute | solution.py:16
  100.5 12.1 %collective-permute-start = (bf16[36,8192]{1,0:T(8,128)(2,1)}, bf16[36,8192]{1,0:T(8,128)(2,1)S(1)}, u32[]{:S(2)}, u32[]{:S(2)}) collective-permute-start(bf16[36,8192]{1,0:T(8,128)(2,1)} %get-tuple-element.1237), channel_id=1, source_target_pairs={{0,16},{16,32},{32,48},{48,64},{64,80},{80,96},{96,112},{1,17},{17... | collective-permute-start | bytes 1769480 | tf_op jit(solution)/shard_map/while/body/eval_jaxpr/ppermute | solution.py:16
  113.5 18.3 %collective-permute-start = (bf16[36,8192]{1,0:T(8,128)(2,1)}, bf16[36,8192]{1,0:T(8,128)(2,1)S(1)}, u32[]{:S(2)}, u32[]{:S(2)}) collective-permute-start(bf16[36,8192]{1,0:T(8,128)(2,1)} %get-tuple-element.1237), channel_id=1, source_target_pairs={{0,16},{16,32},{32,48},{48,64},{64,80},{80,96},{96,112},{1,17},{17... | collective-permute-start | bytes 1769480 | tf_op jit(solution)/shard_map/while/body/eval_jaxpr/ppermute | solution.py:16
  132.8 12.1 %collective-permute-start = (bf16[36,8192]{1,0:T(8,128)(2,1)}, bf16[36,8192]{1,0:T(8,128)(2,1)S(1)}, u32[]{:S(2)}, u32[]{:S(2)}) collective-permute-start(bf16[36,8192]{1,0:T(8,128)(2,1)} %get-tuple-element.1237), channel_id=1, source_target_pairs={{0,16},{16,32},{32,48},{48,64},{64,80},{80,96},{96,112},{1,17},{17... | collective-permute-start | bytes 1769480 | tf_op jit(solution)/shard_map/while/body/eval_jaxpr/ppermute | solution.py:16
  145.8 12.1 %collective-permute-start = (bf16[36,8192]{1,0:T(8,128)(2,1)}, bf16[36,8192]{1,0:T(8,128)(2,1)S(1)}, u32[]{:S(2)}, u32[]{:S(2)}) collective-permute-start(bf16[36,8192]{1,0:T(8,128)(2,1)} %get-tuple-element.1237), channel_id=1, source_target_pairs={{0,16},{16,32},{32,48},{48,64},{64,80},{80,96},{96,112},{1,17},{17... | collective-permute-start | bytes 1769480 | tf_op jit(solution)/shard_map/while/body/eval_jaxpr/ppermute | solution.py:16
  158.8 12.1 %collective-permute-start = (bf16[36,8192]{1,0:T(8,128)(2,1)}, bf16[36,8192]{1,0:T(8,128)(2,1)S(1)}, u32[]{:S(2)}, u32[]{:S(2)}) collective-permute-start(bf16[36,8192]{1,0:T(8,128)(2,1)} %get-tuple-element.1237), channel_id=1, source_target_pairs={{0,16},{16,32},{32,48},{48,64},{64,80},{80,96},{96,112},{1,17},{17... | collective-permute-start | bytes 1769480 | tf_op jit(solution)/shard_map/while/body/eval_jaxpr/ppermute | solution.py:16
  171.8 12.1 %collective-permute-start = (bf16[36,8192]{1,0:T(8,128)(2,1)}, bf16[36,8192]{1,0:T(8,128)(2,1)S(1)}, u32[]{:S(2)}, u32[]{:S(2)}) collective-permute-start(bf16[36,8192]{1,0:T(8,128)(2,1)} %get-tuple-element.1237), channel_id=1, source_target_pairs={{0,16},{16,32},{32,48},{48,64},{64,80},{80,96},{96,112},{1,17},{17... | collective-permute-start | bytes 1769480 | tf_op jit(solution)/shard_map/while/body/eval_jaxpr/ppermute | solution.py:16
  184.8 12.1 %collective-permute-start = (bf16[36,8192]{1,0:T(8,128)(2,1)}, bf16[36,8192]{1,0:T(8,128)(2,1)S(1)}, u32[]{:S(2)}, u32[]{:S(2)}) collective-permute-start(bf16[36,8192]{1,0:T(8,128)(2,1)} %get-tuple-element.1237), channel_id=1, source_target_pairs={{0,16},{16,32},{32,48},{48,64},{64,80},{80,96},{96,112},{1,17},{17... | collective-permute-start | bytes 1769480 | tf_op jit(solution)/shard_map/while/body/eval_jaxpr/ppermute | solution.py:16
  205.8 12.7 %collective-permute-start.1 = (bf16[36,8192]{1,0:T(8,128)(2,1)}, bf16[36,8192]{1,0:T(8,128)(2,1)S(1)}, u32[]{:S(2)}, u32[]{:S(2)}) collective-permute-start(bf16[36,8192]{1,0:T(8,128)(2,1)} %get-tuple-element.1254), channel_id=1, source_target_pairs={{16,0},{32,16},{48,32},{64,48},{80,64},{96,80},{112,96},{17,1},{33... | collective-permute-start | bytes 1769480 | tf_op jit(solution)/shard_map/while/body/eval_jaxpr/ppermute | solution.py:16
  219.4 12.1 %collective-permute-start.1 = (bf16[36,8192]{1,0:T(8,128)(2,1)}, bf16[36,8192]{1,0:T(8,128)(2,1)S(1)}, u32[]{:S(2)}, u32[]{:S(2)}) collective-permute-start(bf16[36,8192]{1,0:T(8,128)(2,1)} %get-tuple-element.1254), channel_id=1, source_target_pairs={{16,0},{32,16},{48,32},{64,48},{80,64},{96,80},{112,96},{17,1},{33... | collective-permute-start | bytes 1769480 | tf_op jit(solution)/shard_map/while/body/eval_jaxpr/ppermute | solution.py:16
  232.4 12.1 %collective-permute-start.1 = (bf16[36,8192]{1,0:T(8,128)(2,1)}, bf16[36,8192]{1,0:T(8,128)(2,1)S(1)}, u32[]{:S(2)}, u32[]{:S(2)}) collective-permute-start(bf16[36,8192]{1,0:T(8,128)(2,1)} %get-tuple-element.1254), channel_id=1, source_target_pairs={{16,0},{32,16},{48,32},{64,48},{80,64},{96,80},{112,96},{17,1},{33... | collective-permute-start | bytes 1769480 | tf_op jit(solution)/shard_map/while/body/eval_jaxpr/ppermute | solution.py:16
  245.4 12.1 %collective-permute-start.1 = (bf16[36,8192]{1,0:T(8,128)(2,1)}, bf16[36,8192]{1,0:T(8,128)(2,1)S(1)}, u32[]{:S(2)}, u32[]{:S(2)}) collective-permute-start(bf16[36,8192]{1,0:T(8,128)(2,1)} %get-tuple-element.1254), channel_id=1, source_target_pairs={{16,0},{32,16},{48,32},{64,48},{80,64},{96,80},{112,96},{17,1},{33... | collective-permute-start | bytes 1769480 | tf_op jit(solution)/shard_map/while/body/eval_jaxpr/ppermute | solution.py:16
  258.4 12.1 %collective-permute-start.1 = (bf16[36,8192]{1,0:T(8,128)(2,1)}, bf16[36,8192]{1,0:T(8,128)(2,1)S(1)}, u32[]{:S(2)}, u32[]{:S(2)}) collective-permute-start(bf16[36,8192]{1,0:T(8,128)(2,1)} %get-tuple-element.1254), channel_id=1, source_target_pairs={{16,0},{32,16},{48,32},{64,48},{80,64},{96,80},{112,96},{17,1},{33... | collective-permute-start | bytes 1769480 | tf_op jit(solution)/shard_map/while/body/eval_jaxpr/ppermute | solution.py:16
  271.4 97.9 %collective-permute-start.1 = (bf16[36,8192]{1,0:T(8,128)(2,1)}, bf16[36,8192]{1,0:T(8,128)(2,1)S(1)}, u32[]{:S(2)}, u32[]{:S(2)}) collective-permute-start(bf16[36,8192]{1,0:T(8,128)(2,1)} %get-tuple-element.1254), channel_id=1, source_target_pairs={{16,0},{32,16},{48,32},{64,48},{80,64},{96,80},{112,96},{17,1},{33... | collective-permute-start | bytes 1769480 | tf_op jit(solution)/shard_map/while/body/eval_jaxpr/ppermute | solution.py:16
  386.9 12.1 %collective-permute-start.1 = (bf16[36,8192]{1,0:T(8,128)(2,1)}, bf16[36,8192]{1,0:T(8,128)(2,1)S(1)}, u32[]{:S(2)}, u32[]{:S(2)}) collective-permute-start(bf16[36,8192]{1,0:T(8,128)(2,1)} %get-tuple-element.1254), channel_id=1, source_target_pairs={{16,0},{32,16},{48,32},{64,48},{80,64},{96,80},{112,96},{17,1},{33... | collective-permute-start | bytes 1769480 | tf_op jit(solution)/shard_map/while/body/eval_jaxpr/ppermute | solution.py:16
  416.6 12.1 %collective-permute-start.1 = (bf16[36,8192]{1,0:T(8,128)(2,1)}, bf16[36,8192]{1,0:T(8,128)(2,1)S(1)}, u32[]{:S(2)}, u32[]{:S(2)}) collective-permute-start(bf16[36,8192]{1,0:T(8,128)(2,1)} %get-tuple-element.1254), channel_id=1, source_target_pairs={{16,0},{32,16},{48,32},{64,48},{80,64},{96,80},{112,96},{17,1},{33... | collective-permute-start | bytes 1769480 | tf_op jit(solution)/shard_map/while/body/eval_jaxpr/ppermute | solution.py:16
  446.3 12.1 %collective-permute-start.1 = (bf16[36,8192]{1,0:T(8,128)(2,1)}, bf16[36,8192]{1,0:T(8,128)(2,1)S(1)}, u32[]{:S(2)}, u32[]{:S(2)}) collective-permute-start(bf16[36,8192]{1,0:T(8,128)(2,1)} %get-tuple-element.1254), channel_id=1, source_target_pairs={{16,0},{32,16},{48,32},{64,48},{80,64},{96,80},{112,96},{17,1},{33... | collective-permute-start | bytes 1769480 | tf_op jit(solution)/shard_map/while/body/eval_jaxpr/ppermute | solution.py:16
  476.0 12.1 %collective-permute-start.1 = (bf16[36,8192]{1,0:T(8,128)(2,1)}, bf16[36,8192]{1,0:T(8,128)(2,1)S(1)}, u32[]{:S(2)}, u32[]{:S(2)}) collective-permute-start(bf16[36,8192]{1,0:T(8,128)(2,1)} %get-tuple-element.1254), channel_id=1, source_target_pairs={{16,0},{32,16},{48,32},{64,48},{80,64},{96,80},{112,96},{17,1},{33... | collective-permute-start | bytes 1769480 | tf_op jit(solution)/shard_map/while/body/eval_jaxpr/ppermute | solution.py:16
  489.0 12.6 %collective-permute-start.1 = (bf16[36,8192]{1,0:T(8,128)(2,1)}, bf16[36,8192]{1,0:T(8,128)(2,1)S(1)}, u32[]{:S(2)}, u32[]{:S(2)}) collective-permute-start(bf16[36,8192]{1,0:T(8,128)(2,1)} %get-tuple-element.1254), channel_id=1, source_target_pairs={{16,0},{32,16},{48,32},{64,48},{80,64},{96,80},{112,96},{17,1},{33... | collective-permute-start | bytes 1769480 | tf_op jit(solution)/shard_map/while/body/eval_jaxpr/ppermute | solution.py:16
  507.4 156.7 %reduce-scatter.5.cloned.1.call-start = ((), (), s32[]{:S(2)}) async-start(), calls=%async_computation.3 | async-start | bytes 4456448 | tf_op jit(solution)/shard_map/reduce_scatter | solution.py:240
  (36 other events, 121.7 us)
Sparse Core Ops, SparseCore 0:
  507.5 75.7 reduce-scatter.2
  587.0 77.0 reduce-scatter.4
where the time goes:
time: 677 us; the launch traced here: 674 us
  waiting for transfers between devices  358 us (53%)
  starting transfers between devices  81 us (12%)
  blocking collectives  66.7 us (10%)
  local copies, waits for them, and re-layouts  60.6 us (9%)
  matrix products  58.7 us (9%)
  other arithmetic  32.2 us (5%)
  between operations  16 us (2%)
    ppermute x22, waiting for transfers between devices, from_behind(): return lax.ppermute(shard, axis, pairs)  276 us
    ppermute x22, starting transfers between devices, from_behind(): return lax.ppermute(shard, axis, pairs)  80.9 us
    reduce_scatter x1, waiting for transfers between devices, local(): lax.psum_scatter(grad_out_sum.astype(jnp.bfloat16), 'dp', scatter_dimensi...  79 us
    psum x1, blocking collectives, local(): objective = lax.psum(loss_local, ('section', 'dp')) / token_count  66.7 us
    cond x56, local copies, waits for them, and re-layouts  23.9 us
    dot_general x4, matrix products, layer_forward(): hidden_pre = jnp.dot(normed, matrix_in, preferred_element_type=jnp.float32)  15.5 us
    dot_general x4, matrix products, layer_backward(): lax.dot_general(grad_rows, matrix_out, (((1,), (1,)), ((), ())), preferre...  14.9 us
    another operation x18, local copies, waits for them, and re-layouts  14.6 us
  transfers between devices with their start and end apart: 24, of which 24 were waited for; matrix products, arithmetic and copies ran while one was open for 1% of the time, Pallas kernels for 0%

commit v1 on v0

v1 whole, which is shorter than its diff:
```python
import functools

import jax
import jax.numpy as jnp
from jax import lax
from jax.experimental import pallas as pl
from jax.experimental.pallas import tpu as pltpu
from jax.sharding import PartitionSpec as P

EPS = 1e-05
LOSS_SCALE = 4096.0
BAL = 16

f32 = jnp.float32
bf16 = jnp.bfloat16
NT = (((1,), (1,)), ((), ()))
TN = (((0,), (0,)), ((), ()))


def mm(a, b, dims=(((1,), (0,)), ((), ()))):
    return lax.dot_general(a, b, dims, preferred_element_type=f32)


def exact(a, b, dims):
    return lax.dot_general(
        a, b, dims, precision=lax.Precision.HIGHEST, preferred_element_type=f32
    )


def split(v, terms):
    out = []
    for _ in range(terms):
        hi = v.astype(bf16)
        out.append(hi)
        v = v - hi.astype(f32)
    return out


def recurrence(layers, width, grad_scale, tiles_ref, rows_ref, side_ref, heads_ref, out_ref, held, sems):
    copies = {}
    for j in range(layers):
        for at in [(k, j) for k in range(j, layers)] + [(j, k) for k in range(j + 1, layers)]:
            copies[at] = pltpu.make_async_copy(
                tiles_ref.at[at[0], :, at[1]], held.at[at[0], at[1]], sems.at[at[0], at[1]]
            )
            copies[at].start()
    adapt = rows_ref.shape[2] // 2
    heads = heads_ref.shape[1]
    tile = lambda k, j: held[k, j].reshape(adapt, adapt)
    side = side_ref[...]
    sq = side[:, 0:1]
    est = [side[:, 1 + k : 2 + k] for k in range(heads)]
    mask = side[:, 4:5]
    target = [side[:, 5 + k : 6 + k] for k in range(heads)]
    coef = [side[:, 8 + k : 9 + k] for k in range(heads)]
    into = [rows_ref[k, :, :adapt] for k in range(layers)]
    onto = [rows_ref[k, :, adapt:] for k in range(layers)]
    pre, fac, kept = [], [], {}
    for j in range(layers):
        for k in range(j, layers):
            copies[k, j].wait()
            if k > j:
                copies[j, k].wait()
        f = lax.rsqrt(jnp.maximum(sq, 0.0) / width + EPS)
        p = f * into[j]
        sg = jax.nn.sigmoid(p)
        act = (p * sg).astype(bf16)
        out_ref[:, j * adapt : (j + 1) * adapt] = act.astype(f32)
        wide = act.astype(f32)
        pre.append(p)
        fac.append(f)
        for k in range(j):
            kept[j, k] = onto[k]
        before = onto[j]
        for k in range(layers):
            if k <= j:
                onto[k] = onto[k] + mm(act, tile(k, j))
            else:
                into[k] = into[k] + mm(act, tile(k, j))
                onto[k] = onto[k] + mm(act, tile(j, k), NT)
        sq = sq + jnp.sum(wide * (before + onto[j]), axis=1, keepdims=True)
        for k in range(heads):
            est[k] = est[k] + jnp.sum(wide * heads_ref[j, k : k + 1, :], axis=1, keepdims=True)
    f = lax.rsqrt(jnp.maximum(sq, 0.0) / width + EPS)
    loss = jnp.zeros_like(sq)
    along = jnp.zeros_like(sq)
    lane = lax.broadcasted_iota(jnp.int32, (side.shape[0], 128), 1)
    extra = jnp.zeros(lane.shape, f32)
    grads = []
    for k in range(heads):
        e = f * est[k]
        err = e - target[k]
        weighted = coef[k] * mask * err
        loss = loss + 0.5 * weighted * err
        scaled = weighted * grad_scale
        along = along + scaled * e
        grads.append(f * scaled)
        extra = jnp.where(lane == layers + k, grads[k], extra)
    extra = jnp.where(lane == layers + heads, loss, extra)
    total = f * f * along / width
    back = []
    for k in range(layers):
        start = -total * onto[k]
        for h in range(heads):
            start = start + grads[h] * heads_ref[k, h : h + 1, :]
        back.append(start)
    for l in range(layers - 1, -1, -1):
        extra = jnp.where(lane == l, total, extra)
        sg = jax.nn.sigmoid(pre[l])
        delta = (fac[l] * (back[l] * sg * (1.0 + pre[l] * (1.0 - sg)))).astype(bf16)
        wide = delta.astype(f32)
        out_ref[:, (layers + l) * adapt : (layers + l + 1) * adapt] = wide
        s = fac[l] / width * jnp.sum(wide * pre[l], axis=1, keepdims=True)
        total = total + s
        for k in range(l):
            back[k] = back[k] + mm(delta, tile(l, k), NT) - s * kept[l, k]
    out_ref[:, 2 * layers * adapt :] = extra


def local(
    hidden,
    lengths,
    response_mask,
    norm_gain,
    weight_in,
    weight_out,
    final_gain,
    value_heads,
    old_values,
    advantages,
    multipliers,
):
    shards = lax.axis_size("dp")
    layers = lax.axis_size("section")
    d = lax.axis_index("dp")
    l = lax.axis_index("section")
    micro, cap, width = hidden.shape
    heads = value_heads.shape[0]
    adapt = weight_in.shape[2]
    total = micro * BAL * shards
    part = width // shards
    own = total // (shards * layers)
    per_micro = total // micro

    gain = norm_gain[0]
    gw = (gain[:, None] * weight_in[0].astype(f32)).astype(bf16)
    wo = weight_out[0]
    wo_sl = lax.dynamic_slice(wo, (0, d * part), (adapt, part))
    gw_sl = lax.dynamic_slice(gw, (d * part, 0), (part, adapt))
    wo_all = lax.all_gather(wo_sl, "section")
    gw_all = lax.all_gather(gw_sl, "section")

    t_in = lax.dot_general(wo_all, gw_sl, (((2,), (0,)), ((), ())), preferred_element_type=f32)
    t_out = lax.dot_general(wo_all, wo_sl, (((2,), (1,)), ((), ())), preferred_element_type=f32)
    tiles = jnp.where(jnp.arange(layers)[:, None, None] < l, t_in, t_out).astype(bf16)
    tiles = lax.psum_scatter(tiles, "dp", scatter_dimension=1, tiled=True)
    tiles = lax.all_gather(tiles, ("section", "dp"))
    tiles = tiles.reshape(layers, shards, layers, adapt // shards, adapt)

    x0 = hidden.reshape(micro * cap, width)
    gfh = final_gain * value_heads
    x0f = x0.astype(f32)
    sq = jnp.sum(x0f * x0f, axis=1, keepdims=True)
    est = exact(x0f, gfh, NT)
    head_out = lax.all_gather(exact(gfh, wo.astype(f32), NT), "section")
    side = split(jnp.concatenate([sq, est], axis=1), 2)
    rows = jnp.concatenate(
        [mm(x0, gw).astype(bf16), mm(x0, wo, NT).astype(bf16)]
        + side
        + [jnp.zeros((micro * cap, 128 - 2 * (1 + heads)), bf16)],
        axis=1,
    )
    ends = jnp.cumsum(lengths, axis=1)
    begins = ends - lengths
    offsets = jnp.arange(cap, dtype=jnp.int32)
    base = (jnp.arange(micro, dtype=jnp.int32) * per_micro)[:, None, None]
    token = jnp.where(
        offsets[None, None, :] < lengths[:, :, None],
        begins[:, :, None] + offsets[None, None, :],
        -1,
    )
    mine = lax.dynamic_index_in_dim(token, d, 1, keepdims=False)
    mine = jnp.where(mine >= 0, mine + base[:, 0], -1).reshape(-1)
    place = (mine // own) % shards * (own * layers) + mine // (own * shards) * own + mine % own
    place = jnp.where(mine >= 0, place, -1)
    onehot = (jnp.arange(total, dtype=jnp.int32)[:, None] == place[None, :]).astype(bf16)
    rows = mm(onehot, rows).astype(bf16)
    rows = lax.psum_scatter(rows, "dp", scatter_dimension=0, tiled=True)
    rows = lax.all_to_all(
        rows.reshape(layers, own, rows.shape[1]), "section", split_axis=0, concat_axis=0
    )
    sides = rows[0, :, 2 * adapt :].astype(f32)
    rows = rows[:, :, : 2 * adapt].astype(f32)
    count = 1 + heads
    sides = sides[:, :count] + sides[:, count : 2 * count]

    first = (l * shards + d) * own
    batch = first // per_micro
    ids = first % per_micro + jnp.arange(own, dtype=jnp.int32)
    slot = lax.dynamic_index_in_dim(token, batch, 0, keepdims=False).reshape(-1)
    pick = (ids[:, None] == slot[None, :]).astype(f32)
    used = lax.dynamic_index_in_dim(response_mask, batch, 0, keepdims=False).astype(f32)
    aims = lax.dynamic_index_in_dim(old_values + advantages, batch, 1, keepdims=False)
    mask = jnp.sum(pick * used[None, :], axis=1, keepdims=True)
    aim = jnp.sum(pick[:, None, :] * aims[None], axis=2)
    coef = jnp.concatenate([jnp.ones((1,), f32), multipliers])
    side = jnp.concatenate(
        [
            sides,
            mask,
            aim,
            jnp.broadcast_to(coef[None], (own, heads)),
            jnp.zeros((own, 128 - 2 - 3 * heads), f32),
        ],
        axis=1,
    )

    vm = pl.BlockSpec(memory_space=pltpu.VMEM)
    state = pl.pallas_call(
        functools.partial(recurrence, layers, float(width), LOSS_SCALE / total),
        out_shape=jax.ShapeDtypeStruct((own, 2 * layers * adapt + 128), f32),
        in_specs=[pl.BlockSpec(memory_space=pl.ANY), vm, vm, vm],
        out_specs=vm,
        scratch_shapes=[
            pltpu.VMEM((layers, layers, shards, adapt // shards, adapt), bf16),
            pltpu.SemaphoreType.DMA((layers, layers)),
        ],
        compiler_params=pltpu.CompilerParams(vmem_limit_bytes=48 * 1024 * 1024),
        cost_estimate=pl.CostEstimate(
            flops=2 * own * adapt * adapt * 128, bytes_accessed=2 * 64 * adapt * adapt, transcendentals=0
        ),
        name="recurrence",
    )(tiles, rows, side, head_out)

    body = state[:, : 2 * layers * adapt].astype(bf16)
    scal = split(state[:, 2 * layers * adapt : 2 * layers * adapt + 16], 3)
    body = jnp.concatenate([body] + scal + [jnp.zeros((own, 80), bf16)], axis=1)
    body = lax.all_gather(body, ("section", "dp"), axis=0, tiled=True)
    scal = body[:, 2 * layers * adapt :].astype(f32)
    scal = scal[:, :16] + scal[:, 16:32] + scal[:, 32:48]

    x = lax.all_to_all(
        x0.reshape(micro * cap, shards, part), "dp", split_axis=1, concat_axis=0
    ).reshape(shards, micro, cap, part)
    x = jnp.swapaxes(x, 0, 1).reshape(micro, shards * cap, part)
    sel = jnp.arange(per_micro, dtype=jnp.int32)[None, :, None] == token.reshape(micro, 1, -1)
    x = lax.dot_general(
        sel.astype(bf16), x, (((2,), (1,)), ((0,), (0,))), preferred_element_type=f32
    )
    x = x.astype(bf16).reshape(total, part)

    acts = body[:, : layers * adapt]
    deltas = body[:, layers * adapt : 2 * layers * adapt]
    act = lax.dynamic_slice(acts, (0, l * adapt), (total, adapt))
    delta = lax.dynamic_slice(deltas, (0, l * adapt), (total, adapt))
    sigma = scal[:, :layers]
    ids = jnp.arange(layers)
    sig_l = jnp.sum(jnp.where(ids[None] == l, sigma, 0.0), axis=1, keepdims=True)
    by = jnp.where(ids[None] <= l, sig_l, sigma)
    by = jnp.repeat(-by, adapt, axis=1)
    later = jnp.repeat((ids > l).astype(bf16), adapt)
    earlier = jnp.repeat((ids < l).astype(f32), adapt)
    t_a = mm(act, (acts.astype(f32) * by).astype(bf16), TN).astype(bf16)
    t_d = (mm(act, deltas, TN).astype(bf16)) * later[None]
    grad_out = mm(t_a, wo_all.reshape(layers * adapt, part))
    grad_out += lax.dot_general(
        t_d.reshape(adapt, layers, adapt),
        gw_all,
        (((1, 2), (0, 2)), ((), ())),
        preferred_element_type=f32,
    )
    gfh_sl = lax.dynamic_slice(gfh, (0, d * part), (heads, part))
    t_h = exact(act.astype(f32), scal[:, layers : layers + heads], TN)
    grad_out += exact(t_h, gfh_sl, (((1,), (0,)), ((), ())))
    grad_out -= mm((act.astype(f32) * sig_l).astype(bf16), x, TN)
    t_i = (mm(acts, delta, TN) * earlier[:, None]).astype(bf16)
    grad_in = mm(x, delta, TN) + mm(wo_all.reshape(layers * adapt, part), t_i, TN)
    grad_in = lax.dynamic_slice(gain, (d * part,), (part,))[:, None] * grad_in
    objective = jnp.sum(scal[:, layers + heads]) / total
    return (grad_in[None], grad_out[None], objective)


def solution(mesh):
    return jax.shard_map(
        local,
        mesh=mesh,
        in_specs=(
            P(None, "dp", None),
            P(),
            P(),
            P("section", None),
            P("section", None, None),
            P("section", None, None),
            P(),
            P(),
            P(),
            P(),
            P(),
        ),
        out_specs=(P("section", "dp", None), P("section", None, "dp"), P()),
        check_vma=False,
    )
```

time: 677 us -> 414 us (0.61)
  waiting for transfers between devices: 358 us -> 273 us
  starting transfers between devices: 81 us -> 11.2 us
  blocking collectives: 66.7 us -> 15.3 us
  local copies, waits for them, and re-layouts: 60.6 us -> 29.9 us
  other arithmetic: 32.2 us -> 11.1 us
  matrix products: 58.7 us -> 49.4 us
  Pallas kernels: 0 us -> 7.49 us
    ppermute x22 -> x0, waiting for transfers between devices: 276 us -> none  [from_behind(): return lax.ppermute(shard, axis, pairs)]
    all_gather x0 -> x4, waiting for transfers between devices: none -> 120 us  [the longest x1 63.2 us: local(): tiles = lax.all_gather(tiles, ('section', 'dp'))]
    ppermute x22 -> x0, starting transfers between devices: 80.9 us -> none  [from_behind(): return lax.ppermute(shard, axis, pairs)]
    psum x1 -> x0, blocking collectives: 66.7 us -> none  [local(): objective = lax.psum(loss_local, ('section', 'dp')) / token_count]
    all_to_all x0 -> x2, waiting for transfers between devices: none -> 40.5 us  [the longest x1 35.7 us: local(): lax.all_to_all(x0.reshape(micro * cap, shards, part), 'dp', split_axis=1,...]
    reduce_scatter x2, waiting for transfers between devices: 81.6 us -> 112 us  [the longest x1 58.3 us: local(): tiles = lax.psum_scatter(tiles, 'dp', scatter_dimension=1, tiled=True)]
    cond x56 -> x0, local copies, waits for them, and re-layouts: 23.9 us -> none
    all_gather x0 -> x1, blocking collectives: none -> 15.3 us  [local(): head_out = lax.all_gather(exact(gfh, wo.astype(f32), NT), 'section')]
  transfers between devices with their start and end apart: 24 -> 8, of which waited for: 24 -> 8; matrix products, arithmetic and copies ran while one was open for 1% -> 15% of each run, Pallas kernels for 0% -> 0%
where the time goes in v1:
time: 414 us
  waiting for transfers between devices  273 us (66%)
  matrix products  49.4 us (12%)
  local copies, waits for them, and re-layouts  29.9 us (7%)
  between operations  16.4 us (4%)
  blocking collectives  15.3 us (4%)
  starting transfers between devices  11.2 us (3%)
  other arithmetic  11.1 us (3%)
  Pallas kernels  7.49 us (2%)
    all_gather x1, waiting for transfers between devices, local(): tiles = lax.all_gather(tiles, ('section', 'dp'))  63.2 us
    reduce_scatter x1, waiting for transfers between devices, local(): tiles = lax.psum_scatter(tiles, 'dp', scatter_dimension=1, tiled=True)  58.3 us
    reduce_scatter x1, waiting for transfers between devices, local(): rows = lax.psum_scatter(rows, 'dp', scatter_dimension=0, tiled=True)  53.2 us
    all_to_all x1, waiting for transfers between devices, local(): lax.all_to_all(x0.reshape(micro * cap, shards, part), 'dp', split_axis=1,...  35.7 us
    all_gather x1, waiting for transfers between devices, local(): body = lax.all_gather(body, ('section', 'dp'), axis=0, tiled=True)  31.6 us
    dot_general x8, matrix products, mm(): return lax.dot_general(a, b, dims, preferred_element_type=f32)  27.4 us
    all_gather x1, waiting for transfers between devices, local(): wo_all = lax.all_gather(wo_sl, 'section')  19.2 us
    all_gather x1, blocking collectives, local(): head_out = lax.all_gather(exact(gfh, wo.astype(f32), NT), 'section')  15.3 us
  transfers between devices with their start and end apart: 8, of which 8 were waited for; matrix products, arithmetic and copies ran while one was open for 15% of the time, Pallas kernels for 0%

profile of v1, /device:TPU:1, one launch (start us, length us, event | category | flops | bytes accessed | tf_op | source)
XLA Modules:
  0.0 413.6 jit_solution(7584736761695144722)
XLA Ops:
  9.0 3.0 copy.66
  16.8 3.1 multiply_reduce_fusion
  20.0 19.2 %all-gather.9.cloned.1.call-done = bf16[8,256,512]{2,1,0:T(8,128)(2,1)} async-done(((bf16[1,256,512]{2,1,0:T(8,128)(2,1)}), bf16[8,256,512]{2,1,0:T(8,128)(2,1)}) %all-gather.9.cloned.1.call-update) | async-done | bytes 2097168 | tf_op jit(solution)/shard_map/all_gather | solution.py:150
  41.5 3.3 select_convert_fusion
  44.9 3.6 convolution_bitcast_fusion.1
  49.5 4.6 %fusion.23 = bf16[144,256]{1,0:T(8,128)(2,1)S(1)} fusion(bf16[144,8192]{1,0:T(8,128)(2,1)} %reshape.214, bf16[1,256,8192]{2,1,0:T(8,128)(2,1)} %param.16), kind=kOutput, calls=%fused_computation.33 | convolution fusion | flops 604016640 | bytes 6627328 | tf_op jit(solution)/shard_map/dot_general | solution.py:21
  57.9 58.3 %reduce-scatter.3.cloned.1.call-done = bf16[8,16,256]{2,1,0:T(8,128)(2,1)} async-done(((bf16[8,256,256]{2,1,0:T(8,128)(2,1)}), bf16[8,16,256]{2,1,0:T(8,128)(2,1)}) %reduce-scatter.3.cloned.1.call-update) | async-done | bytes 65552 | tf_op jit(solution)/shard_map/reduce_scatter | solution.py:156
  118.5 5.5 %fusion.32 = f32[1,3,256]{2,1,0:T(4,128)S(1)} fusion(f32[3,8192]{1,0:T(4,128)S(1)} %broadcast_multiply_fusion, bf16[1,256,8192]{2,1,0:T(8,128)(2,1)} %param.16), kind=kOutput, calls=%fused_computation.36 | convolution fusion | flops 75497472 | bytes 4295680 | tf_op jit(solution)/shard_map/dot_general | solution.py:25
  124.0 15.3 %all-gather.3.heads_ref = f32[8,3,256]{2,1,0:T(4,128)S(1)} all-gather(f32[1,3,256]{2,1,0:T(4,128)S(1)} %fusion.32), channel_id=3, replica_groups=mesh['section'=8,'dp'=16] {'section'}, dimensions={0}, use_global_device_ids=true | all-gather | bytes 27648 | tf_op jit(solution)/shard_map/all_gather | solution.py:165
  139.3 53.2 %reduce-scatter.5.cloned.1.call-done = bf16[64,640]{1,0:T(8,128)(2,1)} async-done(((bf16[1024,640]{1,0:T(8,128)(2,1)}), bf16[64,640]{1,0:T(8,128)(2,1)}) %reduce-scatter.5.cloned.1.call-update) | async-done | bytes 81936 | tf_op jit(solution)/shard_map/reduce_scatter | solution.py:188
  192.5 6.6 %all-to-all-start.1 = ((bf16[8,8,640]{2,1,0:T(8,128)(2,1)}), bf16[8,8,640]{2,1,0:T(8,128)(2,1)S(1)}, u32[]{:S(2)}, u32[]{:S(2)}) async-start(bf16[8,8,640]{2,1,0:T(8,128)(2,1)} %bitcast.98), calls=%async_computation.3 | async-start | bytes 163840 | tf_op jit(solution)/shard_map/all_to_all | solution.py:189
  199.1 4.8 %all-to-all-done.1 = bf16[8,8,640]{2,1,0:T(8,128)(2,1)S(1)} async-done(((bf16[8,8,640]{2,1,0:T(8,128)(2,1)}), bf16[8,8,640]{2,1,0:T(8,128)(2,1)S(1)}, u32[]{:S(2)}, u32[]{:S(2)}) %all-to-all-start.1) | async-done | bytes 81952 | tf_op jit(solution)/shard_map/all_to_all | solution.py:189
  204.2 63.2 %all-gather.13.cloned.1.call-done = bf16[1024,16,256]{2,1,0:T(8,128)(2,1)} async-done(((bf16[8,16,256]{2,1,0:T(8,128)(2,1)}), bf16[1024,16,256]{2,1,0:T(8,128)(2,1)}) %all-gather.13.cloned.1.call-update) | async-done | bytes 8388624 | tf_op jit(solution)/shard_map/all_gather | solution.py:157
  267.4 7.5 %recurrence.1 = f32[8,4224]{1,0:T(8,128)S(1)} custom-call(bf16[8,16,8,16,256]{4,3,2,1,0:T(8,128)(2,1)} %bitcast.92, f32[8,8,512]{2,1,0:T(8,128)S(1)} %slice_convert_fusion.2.rows_ref, f32[8,128]{1,0:T(8,128)S(1)} %concatenate.18.side_ref, f32[8,3,256]{2,1,0:T(4,128)S(1)} %all-gather.3.heads_ref), custom_call_target="tpu_custom_call" | custom-call | flops 134217728 | bytes 8388608 | tf_op jit(solution)/shard_map/recurrence/pallas_call | solution.py:219
  278.4 4.4 %copy.67 = bf16[1,144,16,512]{3,1,0,2:T(8,128)(2,1)} copy(bf16[1,144,16,512]{3,2,1,0:T(8,128)(2,1)} %broadcast_in_dim_reshape_reshape.3) | data formatting | bytes 4718592 | tf_op jit(solution)/shard_map/broadcast_in_dim;reshape;reshape | solution.py:242
  282.9 4.1 all-to-all-start
  288.2 35.7 %all-to-all-done = bf16[1,144,16,512]{3,1,0,2:T(8,128)(2,1)S(1)} async-done(((bf16[1,144,16,512]{3,1,0,2:T(8,128)(2,1)}), bf16[1,144,16,512]{3,1,0,2:T(8,128)(2,1)S(1)}, u32[]{:S(2)}, u32[]{:S(2)}) %all-to-all-start) | async-done | bytes 2359328 | tf_op jit(solution)/shard_map/all_to_all | solution.py:242
  329.6 31.6 %all-gather.11.cloned.1.call-done = bf16[1024,4224]{1,0:T(8,128)(2,1)} async-done(((bf16[8,4224]{1,0:T(8,128)(2,1)}), bf16[1024,4224]{1,0:T(8,128)(2,1)}) %all-gather.11.cloned.1.call-update) | async-done | bytes 8650768 | tf_op jit(solution)/shard_map/all_gather | solution.py:238
  364.2 7.4 %copy.81 = f32[128,8,8,256]{3,1,2,0:T(8,128)} copy(f32[128,8,8,256]{3,2,1,0:T(8,128)S(1)} %bitcast.88) | data formatting | bytes 16777216
  379.7 6.4 %all-gather.15.cloned.1.call-done = bf16[4096,256]{1,0:T(8,128)(2,1)} async-done(((bf16[512,256]{1,0:T(8,128)(2,1)}), bf16[4096,256]{1,0:T(8,128)(2,1)}) %all-gather.15.cloned.1.call-update) | async-done | bytes 2097168 | tf_op jit(solution)/shard_map/all_gather | solution.py:151
  386.0 3.5 convolution_bitcast_fusion
  389.5 6.7 %fusion.19 = f32[256,512]{1,0:T(8,128)S(1)} fusion(f32[256,512]{1,0:T(8,128)S(1)} %fusion.55, f32[256,512]{1,0:T(8,128)} %convolution_bitcast_fusion, bf16[2048,512]{1,0:T(8,128)(2,1)S(1)} %bitcast.93, f32[1024,2048]{1,0:T(8,128)} %bitcast.87, bf16[1024,2048]{1,0:T(8,128)(2,1)} %copy-done, s32[]{:T(128)S(6)} %select_n.120), kind=kOutput, calls=%fused_computation.27 | convolution fusion | flops 1617690624 | bytes 16777220 | tf_op jit(solution)/shard_map/dot_general | solution.py:21
  396.2 3.0 fusion.18
  399.8 5.9 %fusion.21 = f32[1,512,256]{2,1,0:T(8,128)} fusion(f32[512,256]{1,0:T(8,128)} %fusion.44, bf16[2048,512]{1,0:T(8,128)(2,1)S(1)} %bitcast.94, f32[2048]{0:T(1024)S(1)} %bitcast.100, bf16[1024,2048]{1,0:T(8,128)(2,1)} %copy-done.4, s32[]{:T(128)S(6)} %select_n.120, f32[512]{0:T(512)S(1)} %bitcast.103, bf16[1024,4224]{1,0:T(8,128)(2,1)} %all-gather.11.cloned.1.call-done), kind=kOutput, calls=%fused_computation.30 | convolution fusion | flops 1611923456 | bytes 7874564 | tf_op jit(solution)/shard_map/dot_general | solution.py:21
  (124 shorter events, 37.6 us)
Async XLA Ops:
  7.2 4.8 %copy-start.11 = (f32[1,8192]{1,0:T(1,128)S(1)}, f32[1,8192]{1,0:T(1,128)}, u32[]{:S(2)}) copy-start(f32[1,8192]{1,0:T(1,128)} %param.14) | copy-start | bytes 98308
  7.2 32.0 %all-gather.9.cloned.1.call-start = ((), (), s32[]{:S(2)}) async-start(), calls=%async_computation.4 | async-start | bytes 2359296 | tf_op jit(solution)/shard_map/all_gather | solution.py:150
  8.9 107.4 %reduce-scatter.3.cloned.1.call-start = ((), (), s32[]{:S(2)}) async-start(), calls=%async_computation.5 | async-start | bytes 1114112 | tf_op jit(solution)/shard_map/reduce_scatter | solution.py:156
  13.8 6.1 %copy-start.8 = (f32[3,8192]{1,0:T(4,128)S(1)}, f32[3,8192]{1,0:T(4,128)}, u32[]{:S(2)}) copy-start(f32[3,8192]{1,0:T(4,128)} %param.18) | copy-start | bytes 294916
  13.8 6.1 %copy-start.9 = (f32[8192]{0:T(1024)S(1)}, f32[8192]{0:T(1024)}, u32[]{:S(2)}) copy-start(f32[8192]{0:T(1024)} %param.17) | copy-start | bytes 98308
  16.7 24.8 %copy-start.6 = (bf16[1,256,512]{2,1,0:T(8,128)(2,1)S(1)}, bf16[1,256,512]{2,1,0:T(8,128)(2,1)}, u32[]{:S(2)}) copy-start(bf16[1,256,512]{2,1,0:T(8,128)(2,1)} %constant_dynamic-slice_fusion.3) | copy-start | bytes 786436
  16.8 27.9 %copy-start.5 = (bf16[512,256]{1,0:T(8,128)(2,1)}, bf16[512,256]{1,0:T(8,128)(2,1)S(1)}, u32[]{:S(2)}) copy-start(bf16[512,256]{1,0:T(8,128)(2,1)S(1)} %fusion.39) | copy-start | bytes 786436
  41.4 7.0 %copy-start.10 = (s32[4,16]{1,0:T(4,128)S(1)}, s32[4,16]{1,0:T(4,128)}, u32[]{:S(2)}) copy-start(s32[4,16]{1,0:T(4,128)} %param.12) | copy-start | bytes 772
  44.8 147.7 %reduce-scatter.5.cloned.1.call-start = ((), (), s32[]{:S(2)}) async-start(), calls=%async_computation.6 | async-start | bytes 1392640 | tf_op jit(solution)/shard_map/reduce_scatter | solution.py:188
  49.5 4.6 %copy-start.1 = (bf16[144,8192]{1,0:T(8,128)(2,1)S(1)}, bf16[144,8192]{1,0:T(8,128)(2,1)}, u32[]{:S(2)}) copy-start(bf16[144,8192]{1,0:T(8,128)(2,1)} %reshape.214) | copy-start | bytes 7077892
  49.5 4.8 %copy-start.3 = (bf16[1,8192,256]{2,1,0:T(8,128)(2,1)S(1)}, bf16[1,8192,256]{2,1,0:T(8,128)(2,1)}, u32[]{:S(2)}) copy-start(bf16[1,8192,256]{2,1,0:T(8,128)(2,1)} %param.15) | copy-start | bytes 12582916
  55.8 143.3 %copy-start.12 = (f32[2]{0:T(128)S(1)}, f32[2]{0:T(128)}, u32[]{:S(2)}) copy-start(f32[2]{0:T(128)} %param.21) | copy-start | bytes 28
  57.7 209.7 %all-gather.13.cloned.1.call-start = ((), (), s32[]{:S(2)}) async-start(), calls=%async_computation.8 | async-start | bytes 8454144 | tf_op jit(solution)/shard_map/all_gather | solution.py:157
  192.5 11.5 %all-to-all-start.1 = ((bf16[8,8,640]{2,1,0:T(8,128)(2,1)}), bf16[8,8,640]{2,1,0:T(8,128)(2,1)S(1)}, u32[]{:S(2)}, u32[]{:S(2)}) async-start(bf16[8,8,640]{2,1,0:T(8,128)(2,1)} %bitcast.98), calls=%async_computation.3 | async-start | bytes 163840 | tf_op jit(solution)/shard_map/all_to_all | solution.py:189
  199.1 162.1 %all-gather.11.cloned.1.call-start = ((), (), s32[]{:S(2)}) async-start(), calls=%async_computation.7 | async-start | bytes 8718336 | tf_op jit(solution)/shard_map/all_gather | solution.py:238
  282.9 41.0 %all-to-all-start = ((bf16[1,144,16,512]{3,1,0,2:T(8,128)(2,1)}), bf16[1,144,16,512]{3,1,0,2:T(8,128)(2,1)S(1)}, u32[]{:S(2)}, u32[]{:S(2)}) async-start(bf16[1,144,16,512]{3,1,0,2:T(8,128)(2,1)} %copy.67), calls=%async_computation | async-start | bytes 4718592 | tf_op jit(solution)/shard_map/all_to_all | solution.py:242
  287.0 99.1 %all-gather.15.cloned.1.call-start = ((), (), s32[]{:S(2)}) async-start(), calls=%async_computation.9 | async-start | bytes 2359296 | tf_op jit(solution)/shard_map/all_gather | solution.py:151
  362.9 9.5 %slice-start = ((s8[8650752]{0:T(1024)(128)(4,1)}), s8[4194304]{0:T(1024)(128)(4,1)S(1)}, s32[]{:S(2)}) async-start(s8[8650752]{0:T(1024)(128)(4,1)} %bitcast.90), calls=%async_computation.10 | async-start | bytes 8388608
  362.9 9.5 %slice-start.1 = ((s8[8650752]{0:T(1024)(128)(4,1)}), s8[4194304]{0:T(1024)(128)(4,1)S(1)}, s32[]{:S(2)}) async-start(s8[8650752]{0:T(1024)(128)(4,1)} %bitcast.90), calls=%async_computation.11 | async-start | bytes 8388608
  364.2 8.2 %slice-start.2 = ((s8[8650752]{0:T(1024)(128)(4,1)}), s8[262144]{0:T(1024)(128)(4,1)S(1)}, s32[]{:S(2)}) async-start(s8[8650752]{0:T(1024)(128)(4,1)} %bitcast.90), calls=%async_computation.12 | async-start | bytes 524288
  372.4 2.9 copy-start.7
  373.9 3.2 copy-start
  373.9 3.5 copy-start.4
  379.7 9.8 %copy-start.2 = (bf16[8,256,512]{2,1,0:T(8,128)(2,1)S(1)}, bf16[8,256,512]{2,1,0:T(8,128)(2,1)}, u32[]{:S(2)}) copy-start(bf16[8,256,512]{2,1,0:T(8,128)(2,1)} %all-gather.9.cloned.1.call-done) | copy-start | bytes 6291460
Sparse Core Ops, SparseCore 0:
  10.3 28.7 all-gather.8
  44.9 71.3 reduce-scatter.2
  119.8 72.6 reduce-scatter.4
  196.0 71.3 all-gather.12
  275.8 85.3 all-gather.10
  362.8 23.1 all-gather.14
